TPU v7x, 512 devices: a whole 4x8x8 slice. The times are simulated.
512 devices in a mesh: rows: 64 (over z, x, core), cols: 8 (over y).
Axes of the slice: x: 4, y: 8, z: 8, core: 2. Of those that a mesh axis runs over, the one named last changes fastest.
Arguments:
- panel: bfloat16 [131072, 8192], P('rows', 'cols'), may hold values from -100 to 100
- omega: bfloat16 [8192, 128], P('cols'), may hold values from -0.0625 to 0.0625
- order: int32 [128], replicated, may hold values from 0 to 127, each once
Outputs:
- basis: bfloat16 [131072, 128], P('rows')
- coefficients: float32 [8192, 128], P(('cols', 'rows'))
Inputs may be any that keep to these rules, and one draw needn't show every extreme that they name: order holds each of 0 to 127 once.
All inputs are finite; a program needn't handle non-finite values.
Results may differ from a plain program's by a relative error of at most 0.0016.
Values may be sent and summed in bfloat16 or wider, within the bound.
A program may use at most 128 MiB of HBM per device.

v0:
```python
import jax
import jax.numpy as jnp
from jax import lax
from jax.sharding import PartitionSpec as P


def local_gram(rows_part, total_rows):
    return jnp.dot(rows_part.T, rows_part, precision=lax.Precision.HIGHEST) / total_rows


def make_basis(sketch_y, lower):
    return lax.linalg.triangular_solve(
        lower, sketch_y, left_side=False, lower=True, transpose_a=True
    ).astype(jnp.bfloat16)


def body(panel, omega, order):
    width = omega.shape[1]
    total_rows = panel.shape[0] * lax.axis_size("rows")
    picker = (order[None, :] == jnp.arange(width, dtype=jnp.int32)[:, None]).astype(jnp.bfloat16)
    test = jnp.dot(omega, picker, preferred_element_type=jnp.float32).astype(jnp.bfloat16)
    partial_y = jnp.dot(panel, test, preferred_element_type=jnp.float32)
    share_rows = panel.shape[0] // lax.axis_size("cols")
    sketch_y = lax.psum(partial_y, "cols")
    share_y = lax.dynamic_slice_in_dim(sketch_y, lax.axis_index("cols") * share_rows, share_rows, 0)
    gram_part = local_gram(share_y, total_rows)
    lower = jnp.linalg.cholesky(lax.psum(gram_part, ("rows", "cols")))
    basis = make_basis(sketch_y, lower)
    scale = 1.0 / jnp.sqrt(jnp.float32(total_rows))
    product = lax.dot_general(
        panel, basis, (((0,), (0,)), ((), ())), preferred_element_type=jnp.float32
    )
    coefficients = lax.psum_scatter(product * scale, "rows", scatter_dimension=0, tiled=True)
    return (basis, coefficients)


def solution(mesh):
    in_specs = (P("rows", "cols"), P("cols", None), P())
    out_specs = (P("rows", None), P(("cols", "rows"), None))
    return jax.shard_map(body, mesh=mesh, in_specs=in_specs, out_specs=out_specs, check_vma=False)
```

profile of v0, /device:TPU:2, one launch (start us, length us, event | category | flops | bytes accessed | tf_op | source)
XLA Modules:
  0.0 587.4 jit_solution(7401007380953354766)
XLA Ops:
  7.2 0.0 copy-start
  7.2 0.0 all-reduce.5.cloned.1.call-start
  7.2 0.9 copy-done
  8.1 4.9 convolution_bitcast_fusion
  13.0 0.0 all-reduce.5.cloned.1.call-update
  13.0 0.0 all-reduce.7.cloned.1.call-start
  13.1 85.8 %all-reduce.5.cloned.1.call-done = f32[2048,128]{0,1:T(8,128)} async-done(((f32[2048,128]{0,1:T(8,128)}), f32[2048,128]{0,1:T(8,128)}) %all-reduce.5.cloned.1.call-update) | async-done | bytes 1048592 | tf_op jit(solution)/shard_map/psum | solution.py:24
  98.8 1.9 convolution_multiply_fusion.1
  100.7 0.0 all-reduce.7.cloned.1.call-update
  100.8 0.0 all-reduce.9.cloned.1.call-start
  100.8 257.3 %all-reduce.7.cloned.1.call-done = f32[128,128]{0,1:T(8,128)} async-done(((f32[128,128]{0,1:T(8,128)}), f32[128,128]{0,1:T(8,128)}) %all-reduce.7.cloned.1.call-update) | async-done | bytes 65552 | tf_op jit(solution)/shard_map/psum | solution.py:27
  358.1 0.9 copy.9
  359.0 0.9 fusion.4
  359.9 11.7 %cholesky.16 = f32[128,128]{1,0:T(8,128)S(1)} custom-call(f32[128,128]{1,0:T(8,128)S(1)} %fusion.4), custom_call_target="Cholesky" | custom-call | tf_op jit(solution)/shard_map/jit(cholesky)/cholesky | solution.py:27
  371.6 0.6 compare_reduce_fusion
  372.3 0.7 fusion.2
  373.0 9.8 %custom-call.6 = f32[1,128,128]{1,2,0:T(8,128)S(1)} custom-call(f32[1,128,128]{2,1,0:T(8,128)S(1)} %fusion.2), custom_call_target="InvertDiagBlocksLowerTriangular" | custom-call | tf_op jit(solution)/shard_map/triangular_solve | solution.py:12
  382.8 3.0 convolution_convert_fusion
  385.8 0.0 copy-start.1
  385.8 3.9 fusion
  389.7 0.0 all-reduce.9.cloned.1.call-update
  389.8 1.3 dynamic-slice
  391.7 187.5 %all-reduce.9.cloned.1.call-done = f32[1024,128]{0,1:T(8,128)} async-done(((f32[1024,128]{0,1:T(8,128)}), f32[1024,128]{0,1:T(8,128)}) %all-reduce.9.cloned.1.call-update) | async-done | bytes 524304
  579.2 0.9 constant_dynamic-slice_fusion
  580.2 0.7 copy.10
  580.8 0.0 copy-done.1
  (1 shorter events, 0.0 us)
Async XLA Ops:
  7.2 1.0 copy-start
  7.2 91.7 %all-reduce.5.cloned.1.call-start = ((), (), s32[]{:S(2)}) async-start(), calls=%async_computation | async-start | bytes 2097152 | tf_op jit(solution)/shard_map/psum | solution.py:24
  13.0 345.1 %all-reduce.7.cloned.1.call-start = ((), (), s32[]{:S(2)}) async-start(), calls=%async_computation.1 | async-start | bytes 131072 | tf_op jit(solution)/shard_map/psum | solution.py:27
  100.8 478.5 %all-reduce.9.cloned.1.call-start = ((), (), s32[]{:S(2)}) async-start(), calls=%async_computation.2 | async-start | bytes 1048576
  385.8 195.0 %copy-start.1 = (bf16[2048,128]{1,0:T(8,128)(2,1)}, bf16[2048,128]{1,0:T(8,128)(2,1)S(1)}, u32[]{:S(2)}) copy-start(bf16[2048,128]{1,0:T(8,128)(2,1)S(1)} %convolution_convert_fusion) | copy-start | bytes 1572868
Sparse Core Ops, SparseCore 0:
  13.1 85.6 all-reduce.4
  104.4 253.6 all-reduce.6
  389.9 189.3 all-reduce.8
where the time goes:
time: 588 us; the launch traced here: 587 us
  waiting for transfers between devices  531 us (90%)
  other arithmetic  23.7 us (4%)
  between operations  14.5 us (2%)
  matrix products  13.7 us (2%)
    psum x1, waiting for transfers between devices, body(): lower = jnp.linalg.cholesky(lax.psum(gram_part, ('rows', 'cols')))  257 us
    unnamed x4, waiting for transfers between devices  188 us
    psum x1, waiting for transfers between devices, body(): sketch_y = lax.psum(partial_y, 'cols')  85.8 us
    another operation x3, other arithmetic, body(): lower = jnp.linalg.cholesky(lax.psum(gram_part, ('rows', 'cols')))  12.4 us
  transfers between devices with their start and end apart: 3, of which 3 were waited for; matrix products, arithmetic and copies ran while one was open for 0% of the time, Pallas kernels for 0%

commit v1 on v0

v1 whole, which is shorter than its diff:
```python
import functools

import jax
import jax.numpy as jnp
from jax import lax
from jax.experimental import pallas as pl
from jax.experimental.pallas import tpu as pltpu
from jax.sharding import PartitionSpec as P

F32 = jnp.float32
BF16 = jnp.bfloat16
MESH = pl.DeviceIdType.MESH
K = 128
NY = 8
NZ = 8
NG = 8
HIGH = lax.Precision.HIGHEST

RIGHTWARD = ((4, 0), (3, 1), (3, 0), (2, 1), (2, 0), (1, 1), (1, 0))
LEFTWARD = ((4, 1), (5, 0), (5, 1), (6, 0), (6, 1), (7, 0), (7, 1))
CHUNKS = (4, 3, 5, 2, 6, 1, 7, 0)


def wide(v):
    return jnp.broadcast_to(v, (8, K))


def factor_block(rows, done, k):
    lane = lax.broadcasted_iota(jnp.int32, (8, K), 1)
    sub = lax.broadcasted_iota(jnp.int32, (8, K), 0)
    b0 = k // 8
    here = rows[b0]
    inside = (lane >= k) & (lane < k + 8)
    cols = [wide(here[:, k + j : k + j + 1]) for j in range(8)]
    s = {(i, j): wide(cols[j][i : i + 1, :]) for i in range(8) for j in range(i + 1)}
    mod = jnp.where(inside, jnp.where(lane - k == sub, 1.0, 0.0), here)
    a = [wide(mod[i : i + 1, :]) for i in range(8)]
    r, low, b = [], {}, []
    for j in range(8):
        r.append(pltpu.reciprocal(s[j, j], approx=False))
        for i in range(j + 1, 8):
            low[i, j] = s[i, j] * r[j]
        for i in range(j + 1, 8):
            for m in range(j + 1, i + 1):
                s[i, m] = s[i, m] - low[i, j] * s[m, j]
    for j in range(8):
        t = a[j]
        for m in range(j):
            t = t - low[j, m] * b[m]
        b.append(t)
    al = [None] * 8
    for j in reversed(range(8)):
        t = b[j] * r[j]
        for m in range(j + 1, 8):
            t = t - low[m, j] * al[m]
        al[j] = t
    out = jnp.zeros((8, K), F32)
    for j in range(8):
        out = jnp.where(sub == j, b[j] * lax.rsqrt(s[j, j]), out)
    done.append(jnp.where(lane <= sub + k, out, 0.0))
    for i in range(b0 + 1, 16):
        acc = jnp.where(inside, 0.0, rows[i])
        for j in range(8):
            acc = acc - wide(rows[i][:, k + j : k + j + 1]) * al[j]
        rows[i] = acc


def kernel(
    total_rows, panel_hbm, omega_hbm, order_ref, basis_hbm, coef_hbm,
    panel_v, omega_v, py, rr, rl, gram_v, a1, a2, a3, gram_f, yh, zt, zr, c1, w1, c2, w2, c3, basis_v, coef_v,
    panel_sem, omega_sem, out_sem, rs_send, rs_recv, g_send, g_recv, ag_send, ag_recv, z_send, z_recv,
):
    rows_at = lax.axis_index("rows")
    y = lax.axis_index("cols")
    z = rows_at // NG
    g = lax.rem(rows_at, NG)
    x = g // 2
    core = lax.rem(g, 2)
    nx = NG // 2

    def at_y(o):
        return (rows_at, lax.rem(y + o, NY))

    def at_z(o):
        return (lax.rem(z + o, NZ) * NG + g, y)

    def at_g(o):
        return (z * NG + lax.rem(g + o, NG), y)

    def send(src, dst, send_sem, recv_sem, device):
        c = pltpu.make_async_remote_copy(
            src_ref=src, dst_ref=dst, send_sem=send_sem, recv_sem=recv_sem, device_id=device, device_id_type=MESH
        )
        c.start()
        sent.append(c)
        return c

    sent = []
    ch = panel_v.shape[1]
    half = ch // 2

    loads = {}
    om = pltpu.make_async_copy(omega_hbm, omega_v, omega_sem)
    om.start()
    for j in CHUNKS:
        loads[j] = pltpu.make_async_copy(
            panel_hbm.at[pl.ds(pl.multiple_of(lax.rem(y + j, NY) * ch, ch), ch), :], panel_v.at[j], panel_sem.at[j]
        )
        loads[j].start()

    barrier = pltpu.get_barrier_semaphore()
    partners = [at_y(o) for o in range(1, NY)] + [at_z(o) for o in range(1, NZ)] + [at_g(o) for o in range(1, NG)]
    for device in partners:
        pl.semaphore_signal(barrier, inc=1, device_id=device, device_id_type=MESH)

    om.wait()
    picker = (order_ref[...] == lax.broadcasted_iota(jnp.int32, (K, K), 0)).astype(BF16)
    omega_v[...] = jnp.dot(omega_v[...], picker, preferred_element_type=F32).astype(BF16)

    def sketch(j):
        loads[j].wait()
        py[j] = jnp.dot(panel_v[j], omega_v[...], preferred_element_type=F32).reshape(2, half, K)

    right, left = at_y(1), at_y(NY - 1)
    copies_r, copies_l = [], []

    def rs_right(i):
        j, h = RIGHTWARD[i]
        if i >= 2:
            copies_r[i - 2].wait_recv()
            py[j, h] = py[j, h] + rr[i - 2]
        copies_r.append(send(py.at[j, h], rr.at[i], rs_send.at[0, i], rs_recv.at[0, i], right))

    def rs_left(i):
        j, h = LEFTWARD[i]
        if i >= 2:
            copies_l[i - 2].wait_recv()
            py[j, h] = py[j, h] + rl[i - 2]
        copies_l.append(send(py.at[j, h], rl.at[i], rs_send.at[1, i], rs_recv.at[1, i], left))

    sketch(4)
    pl.semaphore_wait(barrier, len(partners))
    rs_right(0)
    rs_left(0)
    sketch(3)
    rs_right(1)
    sketch(5)
    rs_left(1)
    for j in (2, 6, 1, 7, 0):
        sketch(j)
    for i in range(2, 7):
        rs_right(i)
        rs_left(i)
    copies_r[5].wait_recv()
    copies_l[5].wait_recv()
    part_b = py[0, 1] + rr[5]
    part_a = py[0, 0] + rl[5]
    copies_r[6].wait_recv()
    copies_l[6].wait_recv()
    share = jnp.concatenate([part_a + rr[6], part_b + rl[6]], axis=0)

    gram_v[...] = (
        lax.dot_general(share, share, (((0,), (0,)), ((), ())), precision=HIGH, preferred_element_type=F32) / total_rows
    ).reshape(NG, K // NG, K)
    st1 = [
        send(gram_v.at[lax.rem(g + o, NG)], a1.at[o], g_send.at[0, o], g_recv.at[0, o], at_g(o)) for o in range(1, NG)
    ]
    share_hi = share.astype(BF16)
    yh[0, 0] = share_hi.reshape(2, half, K)
    yh[1, 0] = (share - share_hi.astype(F32)).astype(BF16).reshape(2, half, K)

    hops = {}

    def gather_hop(kind, s):
        for way, device in ((0, right), (1, left)):
            src = (NY - s) % NY if way == 0 else s
            dst = NY - 1 - s if way == 0 else s + 1
            for h in (0, 1) if s < 3 else (way,):
                if s > 0:
                    hops[kind, s - 1, way, h].wait_recv()
                i = 2 * s + h
                hops[kind, s, way, h] = send(
                    yh.at[kind, src, h], yh.at[kind, dst, h], ag_send.at[kind, way, i], ag_recv.at[kind, way, i], device
                )

    def finish_gather(kind):
        hops[kind, 2, 0, 1].wait_recv()
        hops[kind, 2, 1, 0].wait_recv()
        hops[kind, 3, 0, 0].wait_recv()
        hops[kind, 3, 1, 1].wait_recv()

    def project(j, first=False):
        term = lax.dot_general(
            yh[0, j].reshape(ch, K), panel_v[j], (((0,), (0,)), ((), ())), preferred_element_type=F32
        )
        zt[...] = term if first else zt[...] + term

    gather_hop(0, 0)
    project(0, True)

    for c in st1:
        c.wait_recv()
    part = gram_v[g]
    for o in range(1, NG):
        part = part + a1[o]
    a2[y] = part
    st2 = [send(a2.at[y], a2.at[y], g_send.at[1, o], g_recv.at[1, o], at_y(o)) for o in range(1, NY)]

    gather_hop(0, 1)
    project(7)
    project(1)

    for c in st2:
        c.wait_recv()
    part = a2[0]
    for o in range(1, NY):
        part = part + a2[o]
    a3[z] = part
    st3 = [send(a3.at[z], a3.at[z], g_send.at[2, o], g_recv.at[2, o], at_z(o)) for o in range(1, NZ)]

    gather_hop(0, 2)
    project(6)
    project(2)

    for c in st3:
        c.wait_recv()
    part = a3[0]
    for o in range(1, NZ):
        part = part + a3[o]
    gram_f[g] = part
    st4 = [send(gram_f.at[g], gram_f.at[g], g_send.at[3, o], g_recv.at[3, o], at_g(o)) for o in range(1, NG)]

    gather_hop(0, 3)
    gather_hop(1, 0)
    finish_gather(0)
    project(5)
    project(3)
    project(4)

    per_z = NG * 16
    for b in range(NZ):
        block = zt[:, b * per_z : (b + 1) * per_z].T.reshape(nx, 2, 16, K)
        for h in range(2):
            for i in range(nx):
                zr[h, i, b] = block[i, h]
    other = (z * NG + g + 1 - 2 * core, y)
    zc = send(zr.at[1 - core], c1, z_send.at[0], z_recv.at[0], other)
    gather_hop(1, 1)

    for c in st4:
        c.wait_recv()
    matrix = gram_f[...].reshape(K, K)
    blocks = [matrix[8 * i : 8 * i + 8, :] for i in range(16)]
    done = []
    for k in range(0, 40, 8):
        factor_block(blocks, done, k)

    zc.wait_recv()
    w1[...] = zr[core] + c1[...]
    zx = [
        send(
            w1.at[lax.rem(x + o, nx)], c2.at[o], z_send.at[o], z_recv.at[o],
            (z * NG + lax.rem(x + o, nx) * 2 + core, y),
        )
        for o in range(1, nx)
    ]
    gather_hop(1, 2)
    for k in range(40, 88, 8):
        factor_block(blocks, done, k)
    total = w1[x]
    for o in range(1, nx):
        zx[o - 1].wait_recv()
        total = total + c2[o]
    w2[...] = total
    zz = [
        send(w2.at[lax.rem(z + o, NZ)], c3.at[o], z_send.at[3 + o], z_recv.at[3 + o], at_z(o)) for o in range(1, NZ)
    ]
    gather_hop(1, 3)
    for k in range(88, 128, 8):
        factor_block(blocks, done, k)

    inverse_t = jnp.concatenate(done, axis=0).T
    inv_hi = inverse_t.astype(BF16)
    inv_lo = (inverse_t - inv_hi.astype(F32)).astype(BF16)
    both = jnp.concatenate([inv_hi, inv_lo], axis=1)
    both = jnp.concatenate([both, both], axis=0)
    finish_gather(1)
    outs = []
    for j in range(NY):
        pair = jnp.concatenate([yh[0, j].reshape(ch, K), yh[1, j].reshape(ch, K)], axis=1)
        res = jnp.dot(pair, both, preferred_element_type=F32)
        basis_v[j] = (res[:, :K] + res[:, K:]).astype(BF16)
        c = pltpu.make_async_copy(
            basis_v.at[j], basis_hbm.at[pl.ds(pl.multiple_of(lax.rem(y + j, NY) * ch, ch), ch), :], out_sem.at[j]
        )
        c.start()
        outs.append(c)

    total = w2[z]
    for o in range(1, NZ):
        zz[o - 1].wait_recv()
        total = total + c3[o]
    scale = 1.0 / jnp.sqrt(jnp.float32(total_rows))
    coef_v[...] = jnp.dot(total, inverse_t, precision=HIGH, preferred_element_type=F32) * scale
    c = pltpu.make_async_copy(coef_v, coef_hbm, out_sem.at[NY])
    c.start()
    outs.append(c)
    for c in outs:
        c.wait()
    for c in sent:
        c.wait_send()


def body(panel, omega, order):
    rows, cols = panel.shape
    ch = rows // NY
    half = ch // 2
    total_rows = rows * lax.axis_size("rows")
    dma = pltpu.SemaphoreType.DMA
    vmem = pltpu.VMEM
    per = K // NG
    return pl.pallas_call(
        functools.partial(kernel, total_rows),
        out_shape=(jax.ShapeDtypeStruct((rows, K), BF16), jax.ShapeDtypeStruct((16, K), F32)),
        in_specs=[
            pl.BlockSpec(memory_space=pl.ANY),
            pl.BlockSpec(memory_space=pl.ANY),
            pl.BlockSpec(memory_space=pltpu.VMEM),
        ],
        out_specs=(pl.BlockSpec(memory_space=pl.ANY), pl.BlockSpec(memory_space=pl.ANY)),
        scratch_shapes=[
            vmem((NY, ch, cols), BF16),
            vmem((cols, K), BF16),
            vmem((NY, 2, half, K), F32),
            vmem((7, half, K), F32),
            vmem((7, half, K), F32),
            vmem((NG, per, K), F32),
            vmem((NG, per, K), F32),
            vmem((NY, per, K), F32),
            vmem((NZ, per, K), F32),
            vmem((NG, per, K), F32),
            vmem((2, NY, 2, half, K), BF16),
            vmem((K, cols), F32),
            vmem((2, NG // 2, NZ, 16, K), F32),
            vmem((NG // 2, NZ, 16, K), F32),
            vmem((NG // 2, NZ, 16, K), F32),
            vmem((NG // 2, NZ, 16, K), F32),
            vmem((NZ, 16, K), F32),
            vmem((NZ, 16, K), F32),
            vmem((NY, ch, K), BF16),
            vmem((16, K), F32),
            dma((NY,)),
            dma,
            dma((NY + 1,)),
            dma((2, 7)),
            dma((2, 7)),
            dma((4, 8)),
            dma((4, 8)),
            dma((2, 2, 8)),
            dma((2, 2, 8)),
            dma((12,)),
            dma((12,)),
        ],
        compiler_params=pltpu.CompilerParams(
            collective_id=0, has_side_effects=True, vmem_limit_bytes=48 * 1024 * 1024
        ),
        cost_estimate=pl.CostEstimate(flops=1_300_000_000, bytes_accessed=5_000_000, transcendentals=0),
    )(panel, omega, order.reshape(1, K))


def solution(mesh):
    in_specs = (P("rows", "cols"), P("cols", None), P())
    out_specs = (P("rows", None), P(("cols", "rows"), None))
    return jax.shard_map(body, mesh=mesh, in_specs=in_specs, out_specs=out_specs, check_vma=False)
```

time: 588 us -> 71 us (0.12)
  the two profiles are of different devices: /device:TPU:2 before, /device:TPU:16 now
where the time goes in v1:
time: 71 us; the launch traced here: 70.8 us
  Pallas kernels  64.9 us (91%)
  local copies, waits for them, and re-layouts  5.18 us (7%)
    pallas_call x1, Pallas kernels, body(): pl.pallas_call(functools.partial(kernel, total_rows), out_shape=(jax.Shap...  64.9 us
    unnamed x8, local copies, waits for them, and re-layouts  5.18 us

profile of v1, /device:TPU:16, one launch (start us, length us, event | category | flops | bytes accessed | tf_op | source)
XLA Modules:
  0.0 70.8 jit_solution(16174005836316279606)
XLA Ops:
  0.6 0.0 copy-start
  0.6 2.2 %copy-done = bf16[2048,1024]{1,0:T(8,128)(2,1)S(1)} copy-done((bf16[2048,1024]{1,0:T(8,128)(2,1)S(1)}, bf16[2048,1024]{1,0:T(8,128)(2,1)}, u32[]{:S(2)}) %copy-start) | copy-done | bytes 4194328
  2.8 0.0 copy-start.1
  2.8 0.9 %copy-done.1 = bf16[1024,128]{1,0:T(8,128)(2,1)S(1)} copy-done((bf16[1024,128]{1,0:T(8,128)(2,1)S(1)}, bf16[1024,128]{1,0:T(8,128)(2,1)}, u32[]{:S(2)}) %copy-start.1) | copy-done | bytes 262168
  3.8 0.0 copy-start.2
  3.8 0.7 copy-done.2
  4.4 64.9 %shard_map.50 = (bf16[2048,128]{1,0:T(8,128)(2,1)S(1)}, f32[16,128]{1,0:T(8,128)S(1)}) custom-call(bf16[2048,1024]{1,0:T(8,128)(2,1)S(1)} %copy-done, bf16[1024,128]{1,0:T(8,128)(2,1)S(1)} %copy-done.1, s32[1,128]{1,0:T(1,128)S(1)} %bitcast.1), custom_call_target="tpu_custom_call" | custom-call | flops 1300000000 | bytes 5000000 | tf_op jit(solution)/shard_map/pallas_call | solution.py:322
  69.4 0.8 %copy.7 = bf16[2048,128]{1,0:T(8,128)(2,1)} copy(bf16[2048,128]{1,0:T(8,128)(2,1)S(1)} %get-tuple-element.4) | data formatting | bytes 1048576
  70.2 0.6 copy.8
Async XLA Ops:
  0.6 2.2 %copy-start = (bf16[2048,1024]{1,0:T(8,128)(2,1)S(1)}, bf16[2048,1024]{1,0:T(8,128)(2,1)}, u32[]{:S(2)}) copy-start(bf16[2048,1024]{1,0:T(8,128)(2,1)} %panel_hbm.1) | copy-start | bytes 12582916
  2.8 0.9 %copy-start.1 = (bf16[1024,128]{1,0:T(8,128)(2,1)S(1)}, bf16[1024,128]{1,0:T(8,128)(2,1)}, u32[]{:S(2)}) copy-start(bf16[1024,128]{1,0:T(8,128)(2,1)} %omega_hbm.1) | copy-start | bytes 786436
  3.8 0.7 copy-start.2

commit v2 on v1

v2 whole, which is shorter than its diff:
```python
import functools

import jax
import jax.numpy as jnp
from jax import lax
from jax.experimental import pallas as pl
from jax.experimental.pallas import tpu as pltpu
from jax.sharding import PartitionSpec as P

F32 = jnp.float32
BF16 = jnp.bfloat16
MESH = pl.DeviceIdType.MESH
K = 128
NY = 8
NZ = 8
NG = 8
HIGH = lax.Precision.HIGHEST

CUTS = 2
RIGHTWARD = tuple(
    (j, h * CUTS + c) for j, h in ((4, 0), (3, 1), (3, 0), (2, 1), (2, 0), (1, 1), (1, 0)) for c in range(CUTS)
)
LEFTWARD = tuple(
    (j, h * CUTS + c) for j, h in ((4, 1), (5, 0), (5, 1), (6, 0), (6, 1), (7, 0), (7, 1)) for c in range(CUTS)
)
AHEAD = 2 * CUTS
CHUNKS = (4, 3, 5, 2, 6, 1, 7, 0)


def wide(v):
    return jnp.broadcast_to(v, (8, K))


def factor_block(rows, done, k):
    lane = lax.broadcasted_iota(jnp.int32, (8, K), 1)
    sub = lax.broadcasted_iota(jnp.int32, (8, K), 0)
    b0 = k // 8
    here = rows[b0]
    inside = (lane >= k) & (lane < k + 8)
    cols = [wide(here[:, k + j : k + j + 1]) for j in range(8)]
    s = {(i, j): cols[j][i : i + 1, :] for i in range(8) for j in range(i + 1)}
    mod = jnp.where(inside, jnp.where(lane - k == sub, 1.0, 0.0), here)
    b = [mod[i : i + 1, :] for i in range(8)]
    r, low = [], {}
    for j in range(8):
        r.append(pltpu.reciprocal(s[j, j], approx=False))
        for i in range(j + 1, 8):
            low[i, j] = s[i, j] * r[j]
        for i in range(j + 1, 8):
            for m in range(j + 1, i + 1):
                s[i, m] = s[i, m] - low[i, j] * s[m, j]
    for j in range(8):
        for i in range(j + 1, 8):
            b[i] = b[i] - low[i, j] * b[j]
    al = [b[j] * r[j] for j in range(8)]
    for j in reversed(range(8)):
        for m in range(j):
            al[m] = al[m] - low[j, m] * al[j]
    out = jnp.zeros((8, K), F32)
    for j in range(8):
        out = jnp.where(sub == j, wide(b[j] * lax.rsqrt(s[j, j])), out)
    done.append(jnp.where(lane <= sub + k, out, 0.0))
    al = [wide(v) for v in al]
    for i in range(b0 + 1, 16):
        t = [wide(rows[i][:, k + j : k + j + 1]) * al[j] for j in range(8)]
        while len(t) > 1:
            t = [t[n] + t[n + 1] for n in range(0, len(t), 2)]
        rows[i] = jnp.where(inside, 0.0, rows[i]) - t[0]


def kernel(
    total_rows, panel_hbm, omega_hbm, order_hbm, basis_ref, coef_ref,
    panel_v, omega_v, order_v, py, rr, rl, gram_v, a1, a2, a3, gram_f, yh, zt, zr, c1, w1, c2, w2, c3,
    panel_sem, omega_sem, order_sem, rs_send, rs_recv, g_send, g_recv, ag_send, ag_recv, z_send, z_recv,
    z_word, x_word,
):
    rows_at = lax.axis_index("rows")
    y = lax.axis_index("cols")
    z = rows_at // NG
    g = lax.rem(rows_at, NG)
    x = g // 2
    core = lax.rem(g, 2)
    nx = NG // 2

    def at_y(o):
        return (rows_at, lax.rem(y + o, NY))

    def at_z(o):
        return (lax.rem(z + o, NZ) * NG + g, y)

    def at_g(o):
        return (z * NG + lax.rem(g + o, NG), y)

    def send(src, dst, send_sem, recv_sem, device):
        c = pltpu.make_async_remote_copy(
            src_ref=src, dst_ref=dst, send_sem=send_sem, recv_sem=recv_sem, device_id=device, device_id_type=MESH
        )
        c.start()
        sent.append(c)
        return c

    sent = []
    ch = panel_v.shape[1]
    half = ch // 2

    barrier = pltpu.get_barrier_semaphore()
    beside_z = (at_z(1), at_z(NZ - 1))
    beside_x = tuple((z * NG + lax.rem(x + o, nx) * 2 + core, y) for o in (1, nx - 1))
    other = (z * NG + g + 1 - 2 * core, y)
    partners = (at_y(1), at_y(NY - 1)) + beside_z + beside_x + (other,)
    for device in partners:
        pl.semaphore_signal(barrier, inc=1, device_id=device, device_id_type=MESH)

    loads = {}
    om = pltpu.make_async_copy(omega_hbm, omega_v, omega_sem)
    om.start()
    od = pltpu.make_async_copy(order_hbm, order_v, order_sem)
    od.start()
    for j in CHUNKS:
        loads[j] = pltpu.make_async_copy(
            panel_hbm.at[pl.ds(pl.multiple_of(lax.rem(y + j, NY) * ch, ch), ch), :], panel_v.at[j], panel_sem.at[j]
        )
        loads[j].start()

    om.wait()
    od.wait()
    picker = (order_v[...] == lax.broadcasted_iota(jnp.int32, (K, K), 0)).astype(BF16)
    omega_v[...] = jnp.dot(omega_v[...], picker, preferred_element_type=F32).astype(BF16)

    def sketch(j):
        loads[j].wait()
        py[j] = jnp.dot(panel_v[j], omega_v[...], preferred_element_type=F32).reshape(2 * CUTS, half // CUTS, K)

    right, left = at_y(1), at_y(NY - 1)
    copies_r, copies_l = [], []

    def rs_right(i):
        j, h = RIGHTWARD[i]
        if i >= AHEAD:
            copies_r[i - AHEAD].wait_recv()
            py[j, h] = py[j, h] + rr[i - AHEAD]
        copies_r.append(send(py.at[j, h], rr.at[i], rs_send.at[0, i], rs_recv.at[0, i], right))

    def rs_left(i):
        j, h = LEFTWARD[i]
        if i >= AHEAD:
            copies_l[i - AHEAD].wait_recv()
            py[j, h] = py[j, h] + rl[i - AHEAD]
        copies_l.append(send(py.at[j, h], rl.at[i], rs_send.at[1, i], rs_recv.at[1, i], left))

    def relay(level):
        for sems, pair, levels in ((z_word, beside_z, 3), (x_word, beside_x, 2)):
            for way in (0, 1):
                if 0 < level <= levels:
                    pl.semaphore_wait(sems.at[level - 1, way], 1)
            for way in (0, 1):
                if level < levels:
                    pl.semaphore_signal(sems.at[level, way], inc=1, device_id=pair[way], device_id_type=MESH)

    sketch(4)
    pl.semaphore_wait(barrier, len(partners))
    for i in range(CUTS):
        rs_right(i)
        rs_left(i)
    sketch(3)
    for i in range(CUTS, AHEAD):
        rs_right(i)
    sketch(5)
    for i in range(CUTS, AHEAD):
        rs_left(i)
    relay(0)
    for j in (2, 6, 1, 7, 0):
        sketch(j)
    last = len(RIGHTWARD)
    for i in range(AHEAD, last):
        rs_right(i)
        rs_left(i)
        if i == AHEAD + 2:
            relay(1)
        if i == AHEAD + 5:
            relay(2)
        if i == AHEAD + 8:
            relay(3)
    parts = [py[0, q] for q in range(AHEAD)]
    for i in range(last - AHEAD, last):
        copies_r[i].wait_recv()
        q = RIGHTWARD[i][1]
        parts[q] = parts[q] + rr[i]
        copies_l[i].wait_recv()
        q = LEFTWARD[i][1]
        parts[q] = parts[q] + rl[i]
    share = jnp.concatenate(parts, axis=0)

    gram_v[...] = (
        lax.dot_general(share, share, (((0,), (0,)), ((), ())), precision=HIGH, preferred_element_type=F32) / total_rows
    ).reshape(NG, K // NG, K)
    st1 = [
        send(gram_v.at[lax.rem(g + o, NG)], a1.at[o], g_send.at[0, o], g_recv.at[0, o], at_g(o)) for o in range(1, NG)
    ]
    share_hi = share.astype(BF16)
    yh[0, 0] = share_hi.reshape(2, half, K)
    yh[1, 0] = (share - share_hi.astype(F32)).astype(BF16).reshape(2, half, K)

    hops = {}

    def gather_hop(kind, s):
        for h in (0, 1):
            for way, device in ((0, right), (1, left)):
                src = (NY - s) % NY if way == 0 else s
                dst = NY - 1 - s if way == 0 else s + 1
                if s > 0:
                    hops[kind, s - 1, way, h].wait_recv()
                if s < 3 or h == way:
                    i = 2 * s + h
                    hops[kind, s, way, h] = send(
                        yh.at[kind, src, h], yh.at[kind, dst, h], ag_send.at[kind, way, i], ag_recv.at[kind, way, i],
                        device,
                    )

    def finish_gather(kind):
        for way in (0, 1):
            hops[kind, 3, way, way].wait_recv()

    def project(j, first=False):
        term = lax.dot_general(
            yh[0, j].reshape(ch, K), panel_v[j], (((0,), (0,)), ((), ())), preferred_element_type=F32
        )
        zt[...] = term if first else zt[...] + term

    gather_hop(0, 0)
    project(0, True)
    for c in st1:
        c.wait_recv()
    part = gram_v[g]
    for o in range(1, NG):
        part = part + a1[o]
    a2[z] = part
    st2 = [send(a2.at[z], a2.at[z], g_send.at[1, o], g_recv.at[1, o], at_z(o)) for o in range(1, NZ)]

    gather_hop(0, 1)
    project(7)
    project(1)
    gather_hop(0, 2)
    project(6)
    project(2)
    for c in st2:
        c.wait_recv()
    part = a2[0]
    for o in range(1, NZ):
        part = part + a2[o]
    a3[y] = part
    st3 = [send(a3.at[y], a3.at[y], g_send.at[2, o], g_recv.at[2, o], at_y(o)) for o in range(1, NY)]

    gather_hop(0, 3)
    gather_hop(1, 0)
    project(5)
    project(3)
    for c in st3:
        c.wait_recv()
    part = a3[0]
    for o in range(1, NY):
        part = part + a3[o]
    gram_f[g] = part
    st4 = [send(gram_f.at[g], gram_f.at[g], g_send.at[3, o], g_recv.at[3, o], at_g(o)) for o in range(1, NG)]

    finish_gather(0)
    project(4)
    per_z = NG * 16
    for b in range(NZ):
        block = zt[:, b * per_z : (b + 1) * per_z].T.reshape(nx, 2, 16, K)
        for h in range(2):
            for i in range(nx):
                zr[h, i, b] = block[i, h]
    zc = send(zr.at[1 - core], c1, z_send.at[0], z_recv.at[0], other)
    gather_hop(1, 1)
    zc.wait_recv()
    w1[...] = zr[core] + c1[...]
    zx = [
        send(
            w1.at[lax.rem(x + o, nx)], c2.at[o], z_send.at[o], z_recv.at[o],
            (z * NG + lax.rem(x + o, nx) * 2 + core, y),
        )
        for o in range(1, nx)
    ]
    for c in st4:
        c.wait_recv()
    matrix = gram_f[...].reshape(K, K)
    blocks = [matrix[8 * i : 8 * i + 8, :] for i in range(16)]
    done = []
    for k in range(0, 16, 8):
        factor_block(blocks, done, k)
    gather_hop(1, 2)
    for k in range(16, 40, 8):
        factor_block(blocks, done, k)
    total = w1[x]
    for o in range(1, nx):
        zx[o - 1].wait_recv()
        total = total + c2[o]
    w2[...] = total
    zz = [
        send(w2.at[lax.rem(z + o, NZ)], c3.at[o], z_send.at[3 + o], z_recv.at[3 + o], at_z(o)) for o in range(1, NZ)
    ]
    for k in range(40, 72, 8):
        factor_block(blocks, done, k)
    gather_hop(1, 3)
    for k in range(72, 128, 8):
        factor_block(blocks, done, k)

    inverse_t = jnp.concatenate(done, axis=0).T
    inv_hi = inverse_t.astype(BF16)
    inv_lo = (inverse_t - inv_hi.astype(F32)).astype(BF16)
    both = jnp.concatenate([inv_hi, inv_lo], axis=1)
    both = jnp.concatenate([both, both], axis=0)
    finish_gather(1)
    for j in range(NY):
        pair = jnp.concatenate([yh[0, j].reshape(ch, K), yh[1, j].reshape(ch, K)], axis=1)
        res = jnp.dot(pair, both, preferred_element_type=F32)
        basis_ref[pl.ds(pl.multiple_of(lax.rem(y + j, NY) * ch, ch), ch), :] = (res[:, :K] + res[:, K:]).astype(BF16)

    total = w2[z]
    for o in range(1, NZ):
        zz[o - 1].wait_recv()
        total = total + c3[o]
    scale = 1.0 / jnp.sqrt(jnp.float32(total_rows))
    coef_ref[...] = jnp.dot(total, inverse_t, precision=HIGH, preferred_element_type=F32) * scale
    for c in sent:
        c.wait_send()


def body(panel, omega, order):
    rows, cols = panel.shape
    ch = rows // NY
    half = ch // 2
    total_rows = rows * lax.axis_size("rows")
    dma = pltpu.SemaphoreType.DMA
    vmem = pltpu.VMEM
    per = K // NG
    return pl.pallas_call(
        functools.partial(kernel, total_rows),
        out_shape=(jax.ShapeDtypeStruct((rows, K), BF16), jax.ShapeDtypeStruct((16, K), F32)),
        in_specs=[
            pl.BlockSpec(memory_space=pltpu.HBM),
            pl.BlockSpec(memory_space=pltpu.HBM),
            pl.BlockSpec(memory_space=pltpu.HBM),
        ],
        out_specs=(pl.BlockSpec(memory_space=vmem), pl.BlockSpec(memory_space=vmem)),
        scratch_shapes=[
            vmem((NY, ch, cols), BF16),
            vmem((cols, K), BF16),
            vmem((1, K), jnp.int32),
            vmem((NY, 2 * CUTS, half // CUTS, K), F32),
            vmem((7 * CUTS, half // CUTS, K), F32),
            vmem((7 * CUTS, half // CUTS, K), F32),
            vmem((NG, per, K), F32),
            vmem((NG, per, K), F32),
            vmem((NY, per, K), F32),
            vmem((NZ, per, K), F32),
            vmem((NG, per, K), F32),
            vmem((2, NY, 2, half, K), BF16),
            vmem((K, cols), F32),
            vmem((2, NG // 2, NZ, 16, K), F32),
            vmem((NG // 2, NZ, 16, K), F32),
            vmem((NG // 2, NZ, 16, K), F32),
            vmem((NG // 2, NZ, 16, K), F32),
            vmem((NZ, 16, K), F32),
            vmem((NZ, 16, K), F32),
            dma((NY,)),
            dma,
            dma,
            dma((2, 7 * CUTS)),
            dma((2, 7 * CUTS)),
            dma((4, 8)),
            dma((4, 8)),
            dma((2, 2, 8)),
            dma((2, 2, 8)),
            dma((12,)),
            dma((12,)),
            pltpu.SemaphoreType.REGULAR((3, 2)),
            pltpu.SemaphoreType.REGULAR((2, 2)),
        ],
        compiler_params=pltpu.CompilerParams(
            collective_id=0, has_side_effects=True, vmem_limit_bytes=48 * 1024 * 1024
        ),
        cost_estimate=pl.CostEstimate(flops=1_300_000_000, bytes_accessed=5_000_000, transcendentals=0),
    )(
        pltpu.with_memory_space_constraint(panel, pltpu.HBM),
        pltpu.with_memory_space_constraint(omega, pltpu.HBM),
        pltpu.with_memory_space_constraint(order.reshape(1, K), pltpu.HBM),
    )


def solution(mesh):
    in_specs = (P("rows", "cols"), P("cols", None), P())
    out_specs = (P("rows", None), P(("cols", "rows"), None))
    return jax.shard_map(body, mesh=mesh, in_specs=in_specs, out_specs=out_specs, check_vma=False)
```

time: 71 us -> 59.9 us (0.84)
  Pallas kernels: 64.9 us -> 57.8 us
  local copies, waits for them, and re-layouts: 5.18 us -> 1.39 us
    pallas_call x1, Pallas kernels: 64.9 us -> 57.8 us  [body(): pl.pallas_call(functools.partial(kernel, total_rows), out_shape=(jax.Shap...]
    unnamed x8 -> x2, local copies, waits for them, and re-layouts: 5.18 us -> 1.39 us
where the time goes in v2:
time: 59.9 us; the launch traced here: 59.8 us
  Pallas kernels  57.8 us (96%)
  local copies, waits for them, and re-layouts  1.39 us (2%)
  between operations  0.64 us (1%)
    pallas_call x1, Pallas kernels, body(): pl.pallas_call(functools.partial(kernel, total_rows), out_shape=(jax.Shap...  57.8 us
    unnamed x2, local copies, waits for them, and re-layouts  1.39 us

profile of v2, /device:TPU:16, one launch (start us, length us, event | category | flops | bytes accessed | tf_op | source)
XLA Modules:
  0.0 59.8 jit_solution(8280711889472834425)
XLA Ops:
  0.6 57.8 %shard_map.50 = (bf16[2048,128]{1,0:T(8,128)(2,1)S(1)}, f32[16,128]{1,0:T(8,128)S(1)}) custom-call(bf16[2048,1024]{1,0:T(8,128)(2,1)} %panel_hbm.1, bf16[1024,128]{1,0:T(8,128)(2,1)} %omega_hbm.1, s32[1,128]{1,0:T(1,128)} %bitcast.1), custom_call_target="tpu_custom_call" | custom-call | flops 1300000000 | bytes 5000000 | tf_op jit(solution)/shard_map/pallas_call | solution.py:338
  58.4 0.8 %copy.7 = bf16[2048,128]{1,0:T(8,128)(2,1)} copy(bf16[2048,128]{1,0:T(8,128)(2,1)S(1)} %get-tuple-element.4) | data formatting | bytes 1048576
  59.2 0.6 %copy.8 = f32[16,128]{1,0:T(8,128)} copy(f32[16,128]{1,0:T(8,128)S(1)} %get-tuple-element.5) | data formatting | bytes 16384

commit v3 on v2

--- a/solution.py
+++ b/solution.py
@@ -204,6 +204,24 @@
     hops = {}
 
     def gather_hop(kind, s):
+        if kind == 1 and s < 3:
+            for way, device in ((0, right), (1, left)):
+                src = (NY - s) % NY if way == 0 else s
+                dst = NY - 1 - s if way == 0 else s + 1
+                if s > 0:
+                    hops[kind, s - 1, way, 0].wait_recv()
+                hops[kind, s, way, 0] = send(
+                    yh.at[kind, src], yh.at[kind, dst], ag_send.at[kind, way, s], ag_recv.at[kind, way, s], device
+                )
+            return
+        if kind == 1:
+            for way, device in ((0, right), (1, left)):
+                hops[kind, 2, way, 0].wait_recv()
+                src = (NY - s) % NY if way == 0 else s
+                hops[kind, s, way, way] = send(
+                    yh.at[kind, src, way], yh.at[kind, 4, way], ag_send.at[kind, way, s], ag_recv.at[kind, way, s], device
+                )
+            return
         for h in (0, 1):
             for way, device in ((0, right), (1, left)):
                 src = (NY - s) % NY if way == 0 else s

time: 59.9 us -> 60.3 us (level)
  no operation moved by 1% of the time
where the time goes in v3:
time: 60.3 us; the launch traced here: 60.1 us
  Pallas kernels  58.1 us (96%)
  local copies, waits for them, and re-layouts  1.39 us (2%)
  between operations  0.64 us (1%)
    pallas_call x1, Pallas kernels, body(): pl.pallas_call(functools.partial(kernel, total_rows), out_shape=(jax.Shap...  58.1 us
    unnamed x2, local copies, waits for them, and re-layouts  1.39 us

profile of v3, /device:TPU:16, one launch (start us, length us, event | category | flops | bytes accessed | tf_op | source)
XLA Modules:
  0.0 60.1 jit_solution(9168480248399203879)
XLA Ops:
  0.6 58.1 %shard_map.50 = (bf16[2048,128]{1,0:T(8,128)(2,1)S(1)}, f32[16,128]{1,0:T(8,128)S(1)}) custom-call(bf16[2048,1024]{1,0:T(8,128)(2,1)} %panel_hbm.1, bf16[1024,128]{1,0:T(8,128)(2,1)} %omega_hbm.1, s32[1,128]{1,0:T(1,128)} %bitcast.1), custom_call_target="tpu_custom_call" | custom-call | flops 1300000000 | bytes 5000000 | tf_op jit(solution)/shard_map/pallas_call | solution.py:356
  58.7 0.8 %copy.7 = bf16[2048,128]{1,0:T(8,128)(2,1)} copy(bf16[2048,128]{1,0:T(8,128)(2,1)S(1)} %get-tuple-element.4) | data formatting | bytes 1048576
  59.5 0.6 copy.8
